TPU v7x, 32 devices: a whole 2x2x4 slice. The times are simulated.
32 devices in a mesh: seq: 8 (over y, x, core), mlp: 4 (over z).
Axes of the slice: x: 2, y: 2, z: 4, core: 2. Of those that a mesh axis runs over, the one named last changes fastest.
Arguments:
- tokens: bfloat16 [8, 4, 256, 1024], P('seq'), may hold values from -6 to 6
- ln_gain: float32 [1024], replicated, may hold values from 0.5 to 1.5
- ln_bias: float32 [1024], replicated, may hold values from -3 to 3
- w_query: bfloat16 [1024, 1024], P(None, 'mlp'), may hold values from -0.1875 to 0.1875
- w_key: bfloat16 [1024, 1024], P(None, 'mlp'), may hold values from -0.1875 to 0.1875
- w_value: bfloat16 [1024, 1024], P(None, 'mlp'), may hold values from -0.1875 to 0.1875
- w_attn_out: bfloat16 [1024, 1024], P('mlp'), may hold values from -6 to 6
- w_in: bfloat16 [1024, 4096], P(None, 'mlp'), may hold values from -0.1875 to 0.1875
- b_in: float32 [4096], P('mlp'), may hold values from -3 to 3
- w_mlp_out: bfloat16 [4096, 1024], P('mlp'), may hold values from -0.09375 to 0.09375
- b_out: float32 [1024], replicated, may hold values from -3 to 3
- cotangent: bfloat16 [8, 4, 256, 1024], P('seq'), may hold values from -6 to 6
Outputs:
- mixed: bfloat16 [8, 4, 256, 1024], P('seq')
- d_tokens: bfloat16 [8, 4, 256, 1024], P('seq')
- d_ln_gain: float32 [1024], replicated
- d_ln_bias: float32 [1024], replicated
- d_w_query: float32 [1024, 1024], P(None, 'mlp')
- d_w_key: float32 [1024, 1024], P(None, 'mlp')
- d_w_value: float32 [1024, 1024], P(None, 'mlp')
- d_w_attn_out: float32 [1024, 1024], P('mlp')
- d_w_in: float32 [1024, 4096], P(None, 'mlp')
- d_b_in: float32 [4096], P('mlp')
- d_w_mlp_out: float32 [4096, 1024], P('mlp')
- d_b_out: float32 [1024], replicated
All inputs are finite; a program needn't handle non-finite values.
Results may differ from a plain program's by a relative error of at most 0.02.
Values may be sent and summed in bfloat16 or wider, within the bound.
No kernel may reach another device: no remote copies, remote signals or barrier semaphores. Data moves between devices by JAX's collectives and lax.ppermute only.
A program may use at most 192 MiB of HBM per device.

v0:
```python
from functools import partial

import jax
import jax.numpy as jnp
from jax import lax
from jax.sharding import PartitionSpec as P

HEAD_DIM = 64
ROT = 32


epsilon = 1e-05
neg_big = -1e30
highest = lax.Precision.HIGHEST


def passed_along(x, axis, by):
    peers = lax.axis_size(axis)
    pairs = [(i, i + by) for i in range(peers) if 0 <= i + by < peers]
    return lax.ppermute(x, axis, pairs)


def rotary_tables(positions, model_width, head_size, rotary):
    column = jnp.arange(model_width, dtype=jnp.int32) % head_size
    pairs = (column // 2).astype(jnp.float32)
    freq = 10000.0 ** (-2.0 * pairs / rotary)
    angle = positions.astype(jnp.float32)[:, None] * freq[None, :]
    active = (column < rotary)[None, :]
    cosine = jnp.where(active, jnp.cos(angle), 1.0)
    sine_table = jnp.where(active, jnp.sin(angle), 0.0)
    row_ids = jnp.arange(model_width, dtype=jnp.int32)[:, None]
    col_ids = jnp.arange(model_width, dtype=jnp.int32)[None, :]
    inside = col_ids % head_size < rotary
    lower = inside & (col_ids % 2 == 0) & (row_ids == col_ids + 1)
    upper = inside & (col_ids % 2 == 1) & (row_ids == col_ids - 1)
    swapper = jnp.where(lower, -1.0, jnp.where(upper, 1.0, 0.0)).astype(jnp.float32)
    return (cosine, sine_table, swapper)


def rotate_rows(vectors, cosine, sine_table, swapper):
    turned = jnp.dot(vectors, swapper, precision=highest)
    return vectors * cosine[:, None, :] + turned * sine_table[:, None, :]


def rotate_back(grads_low, cosine, sine_table, swapper):
    grads_wide = grads_low.astype(jnp.float32)
    turned = jnp.dot(grads_wide * sine_table[:, None, :], swapper.T, precision=highest)
    return grads_wide * cosine[:, None, :] + turned


def probs_and_slopes(
    query_block, key_block, value_block, grad_block, log_block, spread_block, visible, score_scale
):
    raw_scores = (
        jnp.einsum("tshd,ushd->shtu", query_block, key_block, preferred_element_type=jnp.float32)
        * score_scale
    )
    causal_mask = visible[None, None]
    probs = jnp.where(causal_mask, jnp.exp(raw_scores - log_block[..., None]), 0.0)
    grad_probs = jnp.einsum(
        "tshd,ushd->shtu", grad_block, value_block, preferred_element_type=jnp.float32
    )
    slopes = (probs * (grad_probs - spread_block[..., None])).astype(jnp.bfloat16)
    return (probs.astype(jnp.bfloat16), slopes)


def per_device(
    tokens,
    ln_gain,
    ln_bias,
    w_query,
    w_key,
    w_value,
    w_attn_out,
    w_in,
    b_in,
    w_mlp_out,
    b_out,
    cotangent,
):
    tokens_here = tokens[0]
    cot_here = cotangent[0]
    seq_count, row_count, model_width = tokens_here.shape
    inner_width = w_query.shape[1]
    head_count = inner_width // HEAD_DIM
    score_scale = HEAD_DIM ** (-0.5)
    shard_total = lax.axis_size("seq")
    my_shard = lax.axis_index("seq")
    positions = my_shard * row_count + jnp.arange(row_count, dtype=jnp.int32)
    cosine, sine_table, swapper = rotary_tables(positions, inner_width, HEAD_DIM, ROT)
    head_shape = (row_count, seq_count, head_count, HEAD_DIM)
    flat_shape = (row_count, seq_count, inner_width)
    inputs_wide = tokens_here.astype(jnp.float32)
    average = jnp.mean(inputs_wide, -1, keepdims=True)
    centred = inputs_wide - average
    inv_std = lax.rsqrt(jnp.mean(centred * centred, -1, keepdims=True) + epsilon)
    unit = centred * inv_std
    normed = (unit * ln_gain + ln_bias).astype(jnp.bfloat16)
    query_pre = jnp.einsum("std,de->tse", normed, w_query, preferred_element_type=jnp.float32)
    key_pre = jnp.einsum("std,de->tse", normed, w_key, preferred_element_type=jnp.float32)
    query_flat = rotate_rows(query_pre, cosine, sine_table, swapper).astype(jnp.bfloat16)
    keys_flat = rotate_rows(key_pre, cosine, sine_table, swapper).astype(jnp.bfloat16)
    values_flat = jnp.einsum(
        "std,de->tse", normed, w_value, preferred_element_type=jnp.float32
    ).astype(jnp.bfloat16)
    query_heads = query_flat.reshape(head_shape)
    keys_heads = keys_flat.reshape(head_shape)
    values_heads = values_flat.reshape(head_shape)

    def attend_block(state, key_block, value_block, visible):
        running_max, exp_total, weighted = state
        raw_scores = (
            jnp.einsum(
                "tshd,ushd->shtu", query_heads, key_block, preferred_element_type=jnp.float32
            )
            * score_scale
        )
        causal_mask = visible[None, None]
        raw_scores = jnp.where(causal_mask, raw_scores, neg_big)
        new_max = jnp.maximum(running_max, jnp.max(raw_scores, -1))
        block_weights = jnp.where(causal_mask, jnp.exp(raw_scores - new_max[..., None]), 0.0)
        shrink = jnp.exp(running_max - new_max)
        exp_total = exp_total * shrink + jnp.sum(block_weights, -1)
        weighted = weighted * jnp.transpose(shrink, (2, 0, 1))[..., None] + jnp.einsum(
            "shtu,ushd->tshd",
            block_weights.astype(jnp.bfloat16),
            value_block,
            preferred_element_type=jnp.float32,
        )
        return (new_max, exp_total, weighted)

    own_mask = positions[:, None] >= positions[None, :]
    state = (
        jnp.full((seq_count, head_count, row_count), neg_big, jnp.float32),
        jnp.zeros((seq_count, head_count, row_count), jnp.float32),
        jnp.zeros(head_shape, jnp.float32),
    )
    state = attend_block(state, keys_heads, values_heads, own_mask)
    stack_shape = (max(shard_total - 1, 1),) + flat_shape
    empty_stack = jnp.zeros(stack_shape, jnp.bfloat16)

    def forward_step(step, carry):
        state, near_keys, near_values, key_stack, value_stack = carry
        near_keys, near_values = passed_along((near_keys, near_values), "seq", 1)
        visible = jnp.broadcast_to(my_shard >= step, (row_count, row_count))
        state = attend_block(
            state, near_keys.reshape(head_shape), near_values.reshape(head_shape), visible
        )
        key_stack = lax.dynamic_update_index_in_dim(key_stack, near_keys, step - 1, 0)
        value_stack = lax.dynamic_update_index_in_dim(value_stack, near_values, step - 1, 0)
        return (state, near_keys, near_values, key_stack, value_stack)

    state, unused_keys, unused_values, key_stack, value_stack = lax.fori_loop(
        1, shard_total, forward_step, (state, keys_flat, values_flat, empty_stack, empty_stack)
    )
    running_max, exp_total, weighted = state
    log_total = running_max + jnp.log(exp_total)
    attended = weighted / jnp.transpose(exp_total, (2, 0, 1))[..., None]
    attended_low = attended.reshape(flat_shape).astype(jnp.bfloat16)
    attn_part = jnp.einsum(
        "tse,ed->std", attended_low, w_attn_out, preferred_element_type=jnp.float32
    )
    gate_in = jnp.einsum("std,df->stf", normed, w_in, preferred_element_type=jnp.float32) + b_in
    hidden = jax.nn.gelu(gate_in, approximate=True).astype(jnp.bfloat16)
    mlp_part = jnp.einsum("stf,fd->std", hidden, w_mlp_out, preferred_element_type=jnp.float32)
    branches = lax.psum((attn_part + mlp_part).astype(jnp.bfloat16), "mlp").astype(jnp.float32)
    mixed = (inputs_wide + branches + b_out).astype(jnp.bfloat16)
    d_w_attn_out = jnp.einsum(
        "tse,std->ed", attended_low, cot_here, preferred_element_type=jnp.float32
    )
    d_w_mlp_out = jnp.einsum("stf,std->fd", hidden, cot_here, preferred_element_type=jnp.float32)
    d_b_out = jnp.sum(cot_here, (0, 1), dtype=jnp.float32)
    d_attended = jnp.einsum(
        "std,ed->tse", cot_here, w_attn_out, preferred_element_type=jnp.float32
    ).astype(jnp.bfloat16)
    d_hidden = jnp.einsum("std,fd->stf", cot_here, w_mlp_out, preferred_element_type=jnp.float32)
    gelu_value, gelu_pull = jax.vjp(partial(jax.nn.gelu, approximate=True), gate_in)
    d_gate = gelu_pull(d_hidden)[0].astype(jnp.bfloat16)
    d_b_in = jnp.sum(d_gate, (0, 1), dtype=jnp.float32)
    grad_heads = d_attended.reshape(head_shape)
    spread = jnp.transpose(jnp.sum(grad_heads.astype(jnp.float32) * attended, -1), (1, 2, 0))
    probs_low, slopes = probs_and_slopes(
        query_heads, keys_heads, values_heads, grad_heads, log_total, spread, own_mask, score_scale
    )
    d_query = (
        jnp.einsum("shtu,ushd->tshd", slopes, keys_heads, preferred_element_type=jnp.float32)
        * score_scale
    )
    d_keys = (
        jnp.einsum("shtu,tshd->ushd", slopes, query_heads, preferred_element_type=jnp.float32)
        * score_scale
    )
    d_values = jnp.einsum(
        "shtu,tshd->ushd", probs_low, grad_heads, preferred_element_type=jnp.float32
    )

    def earlier_piece(step):
        near_keys = lax.dynamic_index_in_dim(key_stack, step - 1, 0, keepdims=False).reshape(
            head_shape
        )
        near_values = lax.dynamic_index_in_dim(value_stack, step - 1, 0, keepdims=False).reshape(
            head_shape
        )
        visible = jnp.broadcast_to(my_shard >= step, (row_count, row_count))
        piece_probs, piece_slopes = probs_and_slopes(
            query_heads, near_keys, near_values, grad_heads, log_total, spread, visible, score_scale
        )
        query_grad = (
            jnp.einsum(
                "shtu,ushd->tshd", piece_slopes, near_keys, preferred_element_type=jnp.float32
            )
            * score_scale
        )
        return (query_grad, piece_probs, piece_slopes)

    def return_step(index, carry):
        query_grad_total, travelling = carry
        step = shard_total - 1 - index
        query_grad, piece_probs, piece_slopes = earlier_piece(step)
        key_grad = (
            jnp.einsum(
                "shtu,tshd->ushd", piece_slopes, query_heads, preferred_element_type=jnp.float32
            )
            * score_scale
        )
        value_grad = jnp.einsum(
            "shtu,tshd->ushd", piece_probs, grad_heads, preferred_element_type=jnp.float32
        )
        joined = jnp.concatenate([key_grad.reshape(flat_shape), value_grad.reshape(flat_shape)], -1)
        travelling = passed_along((travelling + joined).astype(jnp.bfloat16), "seq", -1).astype(
            jnp.float32
        )
        return (query_grad_total + query_grad, travelling)

    start_travel = jnp.zeros((row_count, seq_count, 2 * inner_width), jnp.float32)
    d_query, travelling = lax.fori_loop(0, shard_total - 1, return_step, (d_query, start_travel))
    d_keys = d_keys + travelling[..., :inner_width].reshape(head_shape)
    d_values = d_values + travelling[..., inner_width:].reshape(head_shape)
    d_query_low = d_query.reshape(flat_shape).astype(jnp.bfloat16)
    d_keys_low = d_keys.reshape(flat_shape).astype(jnp.bfloat16)
    d_values_low = d_values.reshape(flat_shape).astype(jnp.bfloat16)
    d_query_pre = rotate_back(d_query_low, cosine, sine_table, swapper).astype(jnp.bfloat16)
    d_key_pre = rotate_back(d_keys_low, cosine, sine_table, swapper).astype(jnp.bfloat16)
    d_w_query = jnp.einsum("std,tse->de", normed, d_query_pre, preferred_element_type=jnp.float32)
    d_w_key = jnp.einsum("std,tse->de", normed, d_key_pre, preferred_element_type=jnp.float32)
    d_w_value = jnp.einsum("std,tse->de", normed, d_values_low, preferred_element_type=jnp.float32)
    d_w_in = jnp.einsum("std,stf->df", normed, d_gate, preferred_element_type=jnp.float32)
    d_normed_part = jnp.einsum(
        "tse,de->std", d_query_pre, w_query, preferred_element_type=jnp.float32
    )
    d_normed_part = d_normed_part + jnp.einsum(
        "tse,de->std", d_key_pre, w_key, preferred_element_type=jnp.float32
    )
    d_normed_part = d_normed_part + jnp.einsum(
        "tse,de->std", d_values_low, w_value, preferred_element_type=jnp.float32
    )
    d_normed_part = d_normed_part + jnp.einsum(
        "stf,df->std", d_gate, w_in, preferred_element_type=jnp.float32
    )
    d_normed = lax.psum(d_normed_part.astype(jnp.bfloat16), "mlp").astype(jnp.float32)
    d_gain = jnp.sum(d_normed * unit, (0, 1))
    d_bias = jnp.sum(d_normed, (0, 1))
    d_unit = d_normed * ln_gain
    d_inputs = inv_std * (
        d_unit
        - jnp.mean(d_unit, -1, keepdims=True)
        - unit * jnp.mean(d_unit * unit, -1, keepdims=True)
    )
    d_tokens = (cot_here.astype(jnp.float32) + d_inputs).astype(jnp.bfloat16)
    summed = (
        lax.psum(d_gain.astype(jnp.bfloat16), "seq").astype(jnp.float32),
        lax.psum(d_bias.astype(jnp.bfloat16), "seq").astype(jnp.float32),
        lax.psum(d_w_query.astype(jnp.bfloat16), "seq").astype(jnp.float32),
        lax.psum(d_w_key.astype(jnp.bfloat16), "seq").astype(jnp.float32),
        lax.psum(d_w_value.astype(jnp.bfloat16), "seq").astype(jnp.float32),
        lax.psum(d_w_attn_out.astype(jnp.bfloat16), "seq").astype(jnp.float32),
        lax.psum(d_w_in.astype(jnp.bfloat16), "seq").astype(jnp.float32),
        lax.psum(d_b_in.astype(jnp.bfloat16), "seq").astype(jnp.float32),
        lax.psum(d_w_mlp_out.astype(jnp.bfloat16), "seq").astype(jnp.float32),
        lax.psum(d_b_out.astype(jnp.bfloat16), "seq").astype(jnp.float32),
    )
    return (
        mixed[None],
        d_tokens[None],
        summed[0],
        summed[1],
        summed[2],
        summed[3],
        summed[4],
        summed[5],
        summed[6],
        summed[7],
        summed[8],
        summed[9],
    )


def solution(mesh):
    return jax.shard_map(
        per_device,
        mesh=mesh,
        in_specs=(
            P("seq", None, None, None),
            P(),
            P(),
            P(None, "mlp"),
            P(None, "mlp"),
            P(None, "mlp"),
            P("mlp", None),
            P(None, "mlp"),
            P("mlp"),
            P("mlp", None),
            P(),
            P("seq", None, None, None),
        ),
        out_specs=(
            P("seq", None, None, None),
            P("seq", None, None, None),
            P(),
            P(),
            P(None, "mlp"),
            P(None, "mlp"),
            P(None, "mlp"),
            P("mlp", None),
            P(None, "mlp"),
            P("mlp"),
            P("mlp", None),
            P(),
        ),
        check_vma=False,
    )
```

profile of v0, /device:TPU:0, one launch (start us, length us, event | category | flops | bytes accessed | tf_op | source)
XLA Modules:
  0.0 787.0 jit_solution(5758487275462522200)
XLA Ops:
  13.1 3.0 convolution_bitcast_fusion.4
  27.2 161.2 %while.49 = (s32[]{:T(128)}, f32[4,4,256]{2,1,0:T(4,128)S(1)}, f32[4,4,256]{2,1,0:T(4,128)S(1)}, f32[256,4,4,64]{0,3,2,1:T(8,128)}, bf16[256,4,256]{0,2,1:T(8,12...) while((s32[]{:T(128)}, f32[4,4,256]{2,1,0:T(4,128)S(1)}, ...), condition=%wide.region_7.8_spmd, body=%wide.region_4.7_spmd.sunk | while | flops 282603520 | bytes 33292560 | solution.py:153
  29.8 5.3 collective-permute-start.1
  44.5 9.4 %collective-permute-start = (bf16[256,4,256]{0,2,1:T(8,128)(2,1)}, bf16[256,4,256]{0,2,1:T(8,128)(2,1)S(1)}, u32[]{:S(2)}, u32[]{:S(2)}) collective-permute-start(bf16[256,4,256]{0,2,1:T(8,128)(2,1)} %get-tuple-element.918), channel_id=1, source_target_pairs={{0,4},{4,8},{8,12},{12,16},{16,20},{20,24},{24,28},{1,5},{5,9},{9,... | collective-permute-start | bytes 1572872 | tf_op jit(solution)/shard_map/while/body/eval_jaxpr/ppermute | solution.py:20
  53.9 5.2 collective-permute-start.1
  68.5 9.4 %collective-permute-start = (bf16[256,4,256]{0,2,1:T(8,128)(2,1)}, bf16[256,4,256]{0,2,1:T(8,128)(2,1)S(1)}, u32[]{:S(2)}, u32[]{:S(2)}) collective-permute-start(bf16[256,4,256]{0,2,1:T(8,128)(2,1)} %get-tuple-element.918), channel_id=1, source_target_pairs={{0,4},{4,8},{8,12},{12,16},{16,20},{20,24},{24,28},{1,5},{5,9},{9,... | collective-permute-start | bytes 1572872 | tf_op jit(solution)/shard_map/while/body/eval_jaxpr/ppermute | solution.py:20
  77.9 5.2 collective-permute-start.1
  92.5 9.4 %collective-permute-start = (bf16[256,4,256]{0,2,1:T(8,128)(2,1)}, bf16[256,4,256]{0,2,1:T(8,128)(2,1)S(1)}, u32[]{:S(2)}, u32[]{:S(2)}) collective-permute-start(bf16[256,4,256]{0,2,1:T(8,128)(2,1)} %get-tuple-element.918), channel_id=1, source_target_pairs={{0,4},{4,8},{8,12},{12,16},{16,20},{20,24},{24,28},{1,5},{5,9},{9,... | collective-permute-start | bytes 1572872 | tf_op jit(solution)/shard_map/while/body/eval_jaxpr/ppermute | solution.py:20
  101.9 5.2 collective-permute-start.1
  116.5 9.4 %collective-permute-start = (bf16[256,4,256]{0,2,1:T(8,128)(2,1)}, bf16[256,4,256]{0,2,1:T(8,128)(2,1)S(1)}, u32[]{:S(2)}, u32[]{:S(2)}) collective-permute-start(bf16[256,4,256]{0,2,1:T(8,128)(2,1)} %get-tuple-element.918), channel_id=1, source_target_pairs={{0,4},{4,8},{8,12},{12,16},{16,20},{20,24},{24,28},{1,5},{5,9},{9,... | collective-permute-start | bytes 1572872 | tf_op jit(solution)/shard_map/while/body/eval_jaxpr/ppermute | solution.py:20
  125.9 5.2 collective-permute-start.1
  140.5 9.4 %collective-permute-start = (bf16[256,4,256]{0,2,1:T(8,128)(2,1)}, bf16[256,4,256]{0,2,1:T(8,128)(2,1)S(1)}, u32[]{:S(2)}, u32[]{:S(2)}) collective-permute-start(bf16[256,4,256]{0,2,1:T(8,128)(2,1)} %get-tuple-element.918), channel_id=1, source_target_pairs={{0,4},{4,8},{8,12},{12,16},{16,20},{20,24},{24,28},{1,5},{5,9},{9,... | collective-permute-start | bytes 1572872 | tf_op jit(solution)/shard_map/while/body/eval_jaxpr/ppermute | solution.py:20
  149.9 5.2 collective-permute-start.1
  164.5 9.4 %collective-permute-start = (bf16[256,4,256]{0,2,1:T(8,128)(2,1)}, bf16[256,4,256]{0,2,1:T(8,128)(2,1)S(1)}, u32[]{:S(2)}, u32[]{:S(2)}) collective-permute-start(bf16[256,4,256]{0,2,1:T(8,128)(2,1)} %get-tuple-element.918), channel_id=1, source_target_pairs={{0,4},{4,8},{8,12},{12,16},{16,20},{20,24},{24,28},{1,5},{5,9},{9,... | collective-permute-start | bytes 1572872 | tf_op jit(solution)/shard_map/while/body/eval_jaxpr/ppermute | solution.py:20
  173.8 5.2 collective-permute-start.1
  188.4 3.8 multiply_reduce_fusion
  197.6 231.9 %while.50 = (s32[]{:T(128)}, f32[256,4,4,64]{0,3,2,1:T(8,128)}, f32[256,4,512]{0,2,1:T(8,128)}, bf16[7,256,4,256]{1,3,2,0:T(8,128)(2,1)}, s32[]{:T(128)}, /*inde...) while((s32[]{:T(128)}, f32[256,4,4,64]{0,3,2,1:T(8,128)}, ...), condition=%wide.region_11.12_spmd.clone, body=%wide.region_10.11_spmd.clone.sunk | while | flops 684982272 | bytes 77119864 | solution.py:236
  199.7 2.8 fusion.283
  202.4 3.3 fusion.285
  213.4 3.3 fusion.284
  216.7 7.2 collective-permute-done.2
  223.9 2.7 convert_element_type.447
  228.7 2.8 fusion.283
  231.5 3.3 fusion.285
  242.4 3.3 fusion.284
  245.7 12.6 %collective-permute-done.2 = bf16[256,4,512]{0,2,1:T(8,128)(2,1)} collective-permute-done((bf16[256,4,512]{0,2,1:T(8,128)(2,1)}, bf16[256,4,512]{0,2,1:T(8,128)(2,1)}, u32[]{:S(2)}, u32[]{:S(2)}) %collective-permute-start.2) | collective-permute-done | bytes 1048608 | tf_op jit(solution)/shard_map/while/body/eval_jaxpr/ppermute | solution.py:20
  258.3 2.7 convert_element_type.447
  263.1 2.8 fusion.283
  265.9 3.3 fusion.285
  269.6 2.5 multiply_convert_fusion.6
  276.8 3.3 fusion.284
  280.1 11.8 %collective-permute-done.2 = bf16[256,4,512]{0,2,1:T(8,128)(2,1)} collective-permute-done((bf16[256,4,512]{0,2,1:T(8,128)(2,1)}, bf16[256,4,512]{0,2,1:T(8,128)(2,1)}, u32[]{:S(2)}, u32[]{:S(2)}) %collective-permute-start.2) | collective-permute-done | bytes 1048608 | tf_op jit(solution)/shard_map/while/body/eval_jaxpr/ppermute | solution.py:20
  291.9 2.7 convert_element_type.447
  296.7 2.8 fusion.283
  299.5 3.3 fusion.285
  310.4 3.3 fusion.284
  313.7 11.8 %collective-permute-done.2 = bf16[256,4,512]{0,2,1:T(8,128)(2,1)} collective-permute-done((bf16[256,4,512]{0,2,1:T(8,128)(2,1)}, bf16[256,4,512]{0,2,1:T(8,128)(2,1)}, u32[]{:S(2)}, u32[]{:S(2)}) %collective-permute-start.2) | collective-permute-done | bytes 1048608 | tf_op jit(solution)/shard_map/while/body/eval_jaxpr/ppermute | solution.py:20
  325.5 2.7 convert_element_type.447
  330.3 2.8 fusion.283
  333.1 3.3 fusion.285
  336.8 2.5 multiply_convert_fusion.6
  344.0 3.3 fusion.284
  347.3 11.8 %collective-permute-done.2 = bf16[256,4,512]{0,2,1:T(8,128)(2,1)} collective-permute-done((bf16[256,4,512]{0,2,1:T(8,128)(2,1)}, bf16[256,4,512]{0,2,1:T(8,128)(2,1)}, u32[]{:S(2)}, u32[]{:S(2)}) %collective-permute-start.2) | collective-permute-done | bytes 1048608 | tf_op jit(solution)/shard_map/while/body/eval_jaxpr/ppermute | solution.py:20
  359.2 2.7 convert_element_type.447
  363.9 2.8 fusion.283
  366.7 3.3 fusion.285
  377.7 3.3 fusion.284
  381.0 11.8 %collective-permute-done.2 = bf16[256,4,512]{0,2,1:T(8,128)(2,1)} collective-permute-done((bf16[256,4,512]{0,2,1:T(8,128)(2,1)}, bf16[256,4,512]{0,2,1:T(8,128)(2,1)}, u32[]{:S(2)}, u32[]{:S(2)}) %collective-permute-start.2) | collective-permute-done | bytes 1048608 | tf_op jit(solution)/shard_map/while/body/eval_jaxpr/ppermute | solution.py:20
  392.8 2.7 convert_element_type.447
  397.6 2.8 fusion.283
  400.4 3.3 fusion.285
  411.3 3.3 fusion.284
  414.6 11.8 %collective-permute-done.2 = bf16[256,4,512]{0,2,1:T(8,128)(2,1)} collective-permute-done((bf16[256,4,512]{0,2,1:T(8,128)(2,1)}, bf16[256,4,512]{0,2,1:T(8,128)(2,1)}, u32[]{:S(2)}, u32[]{:S(2)}) %collective-permute-start.2) | collective-permute-done | bytes 1048608 | tf_op jit(solution)/shard_map/while/body/eval_jaxpr/ppermute | solution.py:20
  426.4 2.7 convert_element_type.447
  449.2 4.6 bitcast_convert_fusion
  453.8 5.1 fusion.207
  460.3 4.1 bitcast_convert_fusion.1
  468.2 2.8 fusion.71
  480.5 113.0 %all-reduce.6.cloned.1.call-done = (bf16[1024,256]{1,0:T(8,128)(2,1)}, bf16[1024,256]{1,0:T(8,128)(2,1)}, bf16[1024,256]{1,0:T(8,128)(2,1)}, bf16[256,1024]{1,0:...) async-done(((bf16[1024,256]{1,0:T(8,128)(2,1)}, bf16[1024,256]{1,0:T(8,128)(2,1)}, bf16[1024,256]{1,0:T(8,128)(2,1)}, bf16[256,1024]{1,0:T(8,128)(2,1)}, ...) | async-done | bytes 6291472 | tf_op jit(solution)/shard_map/psum | solution.py:273
  593.5 4.2 convert_element_type.287
  604.4 147.7 %all-reduce.8.cloned.1.call-done = (bf16[4,256,1024]{2,1,0:T(8,128)(2,1)}, bf16[4,256,1024]{2,1,0:T(8,128)(2,1)}) async-done(((bf16[4,256,1024]{2,1,0:T(8,128)(2,1)}, bf16[4,256,1024]{2,1,0:T(8,128)(2,1)}), (bf16[4,256,1024]{2,1,0:T(8,128)(2,1)}, bf16[4,256,1024]{2,1,0:T(8,128)(2,1)})) %all-reduce.8.cloned.1.call-update) | async-done | bytes 4194320 | tf_op jit(solution)/shard_map/psum | solution.py:166
  752.1 3.8 fusion.47
  757.8 13.9 %all-reduce = (bf16[1024]{0:T(1024)(128)(2,1)S(1)}, bf16[1024]{0:T(1024)(128)(2,1)S(1)}, bf16[1024]{0:T(1024)(128)(2,1)S(1)}, bf16[1024]{0:T(1024)(128)(2,1)S(1)}) all-reduce(bf16[1024]{0:T(1024)(128)(2,1)S(1)} %get-tuple-element.687, bf16[1024]{0:T(1024)(128)(2,1)S(1)} %reduce_sum.125, ...), channel_id=1, replica_groups=mesh['seq'=8,'mlp'=4] {'seq'}, use_global_device_ids=true, to_apply=%region_16.17 | all-reduce | flops 4096 | bytes 16384 | tf_op jit(solution)/shard_map/psum | solution.py:271
  774.1 5.9 fusion.63
  (351 shorter events, 197.7 us)
Async XLA Ops:
  7.2 446.6 %copy-start = (bf16[1024,1024]{1,0:T(8,128)(2,1)S(1)}, bf16[1024,1024]{1,0:T(8,128)(2,1)}, u32[]{:S(2)}) copy-start(bf16[1024,1024]{1,0:T(8,128)(2,1)} %param.25) | copy-start | bytes 6291460
  7.2 5.8 copy-start.39
  7.2 5.8 copy-start.43
  7.2 586.3 %all-reduce.6.cloned.1.call-start = ((), (), s32[]{:S(2)}) async-start(), calls=%async_computation | async-start | bytes 12582912 | tf_op jit(solution)/shard_map/psum | solution.py:273
  13.0 5.7 copy-start.16
  27.4 7.7 collective-permute-start
  29.8 7.1 collective-permute-start.1
  39.1 5.4 copy-start.24
  44.5 14.6 %collective-permute-start = (bf16[256,4,256]{0,2,1:T(8,128)(2,1)}, bf16[256,4,256]{0,2,1:T(8,128)(2,1)S(1)}, u32[]{:S(2)}, u32[]{:S(2)}) collective-permute-start(bf16[256,4,256]{0,2,1:T(8,128)(2,1)} %get-tuple-element.918), channel_id=1, source_target_pairs={{0,4},{4,8},{8,12},{12,16},{16,20},{20,24},{24,28},{1,5},{5,9},{9,... | collective-permute-start | bytes 1572872 | tf_op jit(solution)/shard_map/while/body/eval_jaxpr/ppermute | solution.py:20
  53.9 7.0 collective-permute-start.1
  63.1 5.5 copy-start.24
  68.5 14.6 %collective-permute-start = (bf16[256,4,256]{0,2,1:T(8,128)(2,1)}, bf16[256,4,256]{0,2,1:T(8,128)(2,1)S(1)}, u32[]{:S(2)}, u32[]{:S(2)}) collective-permute-start(bf16[256,4,256]{0,2,1:T(8,128)(2,1)} %get-tuple-element.918), channel_id=1, source_target_pairs={{0,4},{4,8},{8,12},{12,16},{16,20},{20,24},{24,28},{1,5},{5,9},{9,... | collective-permute-start | bytes 1572872 | tf_op jit(solution)/shard_map/while/body/eval_jaxpr/ppermute | solution.py:20
  77.9 7.0 collective-permute-start.1
  87.1 5.4 copy-start.24
  92.5 14.6 %collective-permute-start = (bf16[256,4,256]{0,2,1:T(8,128)(2,1)}, bf16[256,4,256]{0,2,1:T(8,128)(2,1)S(1)}, u32[]{:S(2)}, u32[]{:S(2)}) collective-permute-start(bf16[256,4,256]{0,2,1:T(8,128)(2,1)} %get-tuple-element.918), channel_id=1, source_target_pairs={{0,4},{4,8},{8,12},{12,16},{16,20},{20,24},{24,28},{1,5},{5,9},{9,... | collective-permute-start | bytes 1572872 | tf_op jit(solution)/shard_map/while/body/eval_jaxpr/ppermute | solution.py:20
  101.9 7.0 collective-permute-start.1
  111.1 5.4 copy-start.24
  116.5 14.5 %collective-permute-start = (bf16[256,4,256]{0,2,1:T(8,128)(2,1)}, bf16[256,4,256]{0,2,1:T(8,128)(2,1)S(1)}, u32[]{:S(2)}, u32[]{:S(2)}) collective-permute-start(bf16[256,4,256]{0,2,1:T(8,128)(2,1)} %get-tuple-element.918), channel_id=1, source_target_pairs={{0,4},{4,8},{8,12},{12,16},{16,20},{20,24},{24,28},{1,5},{5,9},{9,... | collective-permute-start | bytes 1572872 | tf_op jit(solution)/shard_map/while/body/eval_jaxpr/ppermute | solution.py:20
  125.9 7.0 collective-permute-start.1
  135.0 5.4 copy-start.24
  140.5 14.5 %collective-permute-start = (bf16[256,4,256]{0,2,1:T(8,128)(2,1)}, bf16[256,4,256]{0,2,1:T(8,128)(2,1)S(1)}, u32[]{:S(2)}, u32[]{:S(2)}) collective-permute-start(bf16[256,4,256]{0,2,1:T(8,128)(2,1)} %get-tuple-element.918), channel_id=1, source_target_pairs={{0,4},{4,8},{8,12},{12,16},{16,20},{20,24},{24,28},{1,5},{5,9},{9,... | collective-permute-start | bytes 1572872 | tf_op jit(solution)/shard_map/while/body/eval_jaxpr/ppermute | solution.py:20
  149.9 7.0 collective-permute-start.1
  159.0 5.4 copy-start.24
  164.5 14.5 %collective-permute-start = (bf16[256,4,256]{0,2,1:T(8,128)(2,1)}, bf16[256,4,256]{0,2,1:T(8,128)(2,1)S(1)}, u32[]{:S(2)}, u32[]{:S(2)}) collective-permute-start(bf16[256,4,256]{0,2,1:T(8,128)(2,1)} %get-tuple-element.918), channel_id=1, source_target_pairs={{0,4},{4,8},{8,12},{12,16},{16,20},{20,24},{24,28},{1,5},{5,9},{9,... | collective-permute-start | bytes 1572872 | tf_op jit(solution)/shard_map/while/body/eval_jaxpr/ppermute | solution.py:20
  173.8 7.0 collective-permute-start.1
  183.0 5.4 copy-start.24
  188.4 3.9 copy-start.6
  188.4 3.9 copy-start.38
  192.3 3.9 copy-start.15
  202.4 3.6 copy-start.2
  202.4 3.7 copy-start.11
  206.1 4.6 copy-start.3
  212.1 11.8 %collective-permute-start.2 = (bf16[256,4,512]{0,2,1:T(8,128)(2,1)}, bf16[256,4,512]{0,2,1:T(8,128)(2,1)}, u32[]{:S(2)}, u32[]{:S(2)}) collective-permute-start(bf16[256,4,512]{0,2,1:T(8,128)(2,1)} %fusion.286), channel_id=1, source_target_pairs={{4,0},{8,4},{12,8},{16,12},{20,16},{24,20},{28,24},{5,1},{9,5},{13... | collective-permute-start | bytes 3145736 | tf_op jit(solution)/shard_map/while/body/eval_jaxpr/ppermute | solution.py:20
  231.5 3.6 copy-start.2
  231.5 3.7 copy-start.11
  235.2 4.6 copy-start.3
  241.1 17.2 %collective-permute-start.2 = (bf16[256,4,512]{0,2,1:T(8,128)(2,1)}, bf16[256,4,512]{0,2,1:T(8,128)(2,1)}, u32[]{:S(2)}, u32[]{:S(2)}) collective-permute-start(bf16[256,4,512]{0,2,1:T(8,128)(2,1)} %fusion.286), channel_id=1, source_target_pairs={{4,0},{8,4},{12,8},{16,12},{20,16},{24,20},{28,24},{5,1},{9,5},{13... | collective-permute-start | bytes 3145736 | tf_op jit(solution)/shard_map/while/body/eval_jaxpr/ppermute | solution.py:20
  265.9 3.6 copy-start.2
  265.9 3.7 copy-start.11
  269.6 4.6 copy-start.3
  275.5 16.4 %collective-permute-start.2 = (bf16[256,4,512]{0,2,1:T(8,128)(2,1)}, bf16[256,4,512]{0,2,1:T(8,128)(2,1)}, u32[]{:S(2)}, u32[]{:S(2)}) collective-permute-start(bf16[256,4,512]{0,2,1:T(8,128)(2,1)} %fusion.286), channel_id=1, source_target_pairs={{4,0},{8,4},{12,8},{16,12},{20,16},{24,20},{28,24},{5,1},{9,5},{13... | collective-permute-start | bytes 3145736 | tf_op jit(solution)/shard_map/while/body/eval_jaxpr/ppermute | solution.py:20
  299.5 3.6 copy-start.2
  299.5 3.7 copy-start.11
  303.2 4.6 copy-start.3
  309.1 16.4 %collective-permute-start.2 = (bf16[256,4,512]{0,2,1:T(8,128)(2,1)}, bf16[256,4,512]{0,2,1:T(8,128)(2,1)}, u32[]{:S(2)}, u32[]{:S(2)}) collective-permute-start(bf16[256,4,512]{0,2,1:T(8,128)(2,1)} %fusion.286), channel_id=1, source_target_pairs={{4,0},{8,4},{12,8},{16,12},{20,16},{24,20},{28,24},{5,1},{9,5},{13... | collective-permute-start | bytes 3145736 | tf_op jit(solution)/shard_map/while/body/eval_jaxpr/ppermute | solution.py:20
  333.1 3.6 copy-start.2
  333.1 3.7 copy-start.11
  336.8 4.6 copy-start.3
  342.8 16.4 %collective-permute-start.2 = (bf16[256,4,512]{0,2,1:T(8,128)(2,1)}, bf16[256,4,512]{0,2,1:T(8,128)(2,1)}, u32[]{:S(2)}, u32[]{:S(2)}) collective-permute-start(bf16[256,4,512]{0,2,1:T(8,128)(2,1)} %fusion.286), channel_id=1, source_target_pairs={{4,0},{8,4},{12,8},{16,12},{20,16},{24,20},{28,24},{5,1},{9,5},{13... | collective-permute-start | bytes 3145736 | tf_op jit(solution)/shard_map/while/body/eval_jaxpr/ppermute | solution.py:20
  366.7 3.6 copy-start.2
  366.7 3.7 copy-start.11
  370.4 4.6 copy-start.3
  376.4 16.4 %collective-permute-start.2 = (bf16[256,4,512]{0,2,1:T(8,128)(2,1)}, bf16[256,4,512]{0,2,1:T(8,128)(2,1)}, u32[]{:S(2)}, u32[]{:S(2)}) collective-permute-start(bf16[256,4,512]{0,2,1:T(8,128)(2,1)} %fusion.286), channel_id=1, source_target_pairs={{4,0},{8,4},{12,8},{16,12},{20,16},{24,20},{28,24},{5,1},{9,5},{13... | collective-permute-start | bytes 3145736 | tf_op jit(solution)/shard_map/while/body/eval_jaxpr/ppermute | solution.py:20
  400.4 3.6 copy-start.2
  400.4 3.7 copy-start.11
  404.1 4.6 copy-start.3
  410.0 16.4 %collective-permute-start.2 = (bf16[256,4,512]{0,2,1:T(8,128)(2,1)}, bf16[256,4,512]{0,2,1:T(8,128)(2,1)}, u32[]{:S(2)}, u32[]{:S(2)}) collective-permute-start(bf16[256,4,512]{0,2,1:T(8,128)(2,1)} %fusion.286), channel_id=1, source_target_pairs={{4,0},{8,4},{12,8},{16,12},{20,16},{24,20},{28,24},{5,1},{9,5},{13... | collective-permute-start | bytes 3145736 | tf_op jit(solution)/shard_map/while/body/eval_jaxpr/ppermute | solution.py:20
  443.0 3.7 copy-start.41
  449.2 4.7 copy-start.45
  464.4 287.7 %all-reduce.8.cloned.1.call-start = ((), (), s32[]{:S(2)}) async-start(), calls=%async_computation.1 | async-start | bytes 8388608 | tf_op jit(solution)/shard_map/psum | solution.py:166
  593.5 4.2 copy-start.20
  597.7 4.6 copy-start.31
  597.7 5.6 copy-start.30
  603.3 170.8 %copy-start.40 = (f32[1024]{0:T(1024)S(1)}, f32[1024]{0:T(1024)}, u32[]{:S(2)}) copy-start(f32[1024]{0:T(1024)} %param.26) | copy-start | bytes 12292
  (44 other events, 92.7 us)
Sparse Core Ops, SparseCore 0:
  464.6 128.8 all-reduce.5
  596.6 155.4 all-reduce.7
where the time goes:
time: 797 us; the launch traced here: 787 us
  waiting for transfers between devices  340 us (43%)
  matrix products  170 us (21%)
  starting transfers between devices  104 us (13%)
  local copies, waits for them, and re-layouts  74.8 us (9%)
  other arithmetic  68.9 us (9%)
  between operations  14.9 us (2%)
  blocking collectives  13.9 us (2%)
    psum x1, waiting for transfers between devices, per_device(): lax.psum((attn_part + mlp_part).astype(jnp.bfloat16), 'mlp')  148 us
    psum x1, waiting for transfers between devices, per_device(): lax.psum(d_w_query.astype(jnp.bfloat16), 'seq').astype(jnp.float32)  113 us
    ppermute x21, starting transfers between devices, passed_along(): return lax.ppermute(x, axis, pairs)  104 us
    ppermute x21, waiting for transfers between devices, passed_along(): return lax.ppermute(x, axis, pairs)  79 us
    while x105, local copies, waits for them, and re-layouts  31.1 us
    dot_general x7, matrix products, earlier_piece(): jnp.einsum('shtu,ushd->tshd', piece_slopes, near_keys, preferred_element_...  23.1 us
    dot_general x7, matrix products, return_step(): jnp.einsum('shtu,tshd->ushd', piece_probs, grad_heads, preferred_element_...  23.1 us
    dot_general x8, matrix products, probs_and_slopes(): jnp.einsum('tshd,ushd->shtu', grad_block, value_block, preferred_element_...  20.2 us
  transfers between devices with their start and end apart: 23, of which 9 were waited for; matrix products, arithmetic and copies ran while one was open for 8% of the time, Pallas kernels for 0%

commit v1 on v0

v1 whole, which is shorter than its diff:
```python
from functools import partial

import jax
import jax.numpy as jnp
from jax import lax
from jax.experimental import pallas as pl
from jax.experimental.pallas import tpu as pltpu
from jax.sharding import PartitionSpec as P

HEAD_DIM = 64
ROT = 32

epsilon = 1e-05
neg_big = -1e30
bf16 = jnp.bfloat16
f32 = jnp.float32


def passed_along(x, axis, by):
    peers = lax.axis_size(axis)
    pairs = [(i, i + by) for i in range(peers) if 0 <= i + by < peers]
    return lax.ppermute(x, axis, pairs)


def rotary_tables(positions, width):
    column = jnp.arange(width, dtype=jnp.int32) % HEAD_DIM
    pairs = (column // 2).astype(f32)
    freq = 10000.0 ** (-2.0 * pairs / ROT)
    angle = positions.astype(f32)[:, None] * freq[None, :]
    active = (column < ROT)[None, :]
    even = (column % 2 == 0)[None, :]
    cosine = jnp.where(active, jnp.cos(angle), 1.0)
    sine = jnp.where(active, jnp.sin(angle), 0.0)
    return cosine, jnp.where(even, -sine, 0.0), jnp.where(even, 0.0, sine)


def rotate(v, tables, sign):
    cosine, from_right, from_left = tables
    right = jnp.concatenate([v[..., 1:], v[..., :1]], -1)
    left = jnp.concatenate([v[..., -1:], v[..., :-1]], -1)
    return v * cosine + sign * (right * from_right + left * from_left)


def attention_kernel(x_ref, out_ref, xt, acc, sbuf, *, length, hd, tq, tk):
    xt[...] = x_ref[0].T
    acc[...] = jnp.zeros_like(acc)
    scale = hd**-0.5
    nt = (((1,), (1,)), ((), ()))
    zero = jnp.zeros((hd, tq), bf16)
    for i in range(length // tq):
        cols = slice(i * tq, (i + 1) * tq)
        span = (i + 1) * tq
        qs = (xt[0:hd, cols].astype(f32) * scale).astype(bf16)
        at = xt[3 * hd : 4 * hd, cols].astype(f32)
        zq = jnp.concatenate([zero, qs], 0)
        qz = jnp.concatenate([qs, zero], 0)
        steps = [(k0, min(k0 + tk, span)) for k0 in range(0, span, tk)]
        top = None
        for k0, k1 in steps:
            st = jnp.dot(x_ref[0, k0:k1, 0 : 2 * hd], zq, preferred_element_type=f32)
            if k1 > i * tq:
                kp = lax.broadcasted_iota(jnp.int32, st.shape, 0) + k0
                qp = lax.broadcasted_iota(jnp.int32, st.shape, 1) + i * tq
                st = jnp.where(kp <= qp, st, neg_big)
            sbuf[k0:k1, :] = st
            m = jnp.max(st, 0, keepdims=True)
            top = m if top is None else jnp.maximum(top, m)
        tot = None
        ot = None
        for k0, k1 in steps:
            e = jnp.exp(sbuf[k0:k1, :] - top)
            sbuf[k0:k1, :] = e
            s = jnp.sum(e, 0, keepdims=True)
            o = jnp.dot(xt[2 * hd : 3 * hd, k0:k1], e.astype(bf16), preferred_element_type=f32)
            tot = s if tot is None else tot + s
            ot = o if ot is None else ot + o
        r = 1.0 / tot
        ot = ot * r
        ar = (at * r).astype(bf16)
        spread = jnp.sum(ar.astype(f32) * ot, 0, keepdims=True)
        az = jnp.concatenate([ar, zero], 0)
        za = jnp.concatenate([zero, ar], 0)
        dqt = None
        for k0, k1 in steps:
            dp = jnp.dot(x_ref[0, k0:k1, 2 * hd : 4 * hd], az, preferred_element_type=f32)
            e = sbuf[k0:k1, :]
            ds = (e * (dp - spread)).astype(bf16)
            d = jnp.dot(xt[hd : 2 * hd, k0:k1], ds, preferred_element_type=f32)
            dqt = d if dqt is None else dqt + d
            acc[k0:k1, :] += lax.dot_general(ds, qz, nt, preferred_element_type=f32) + lax.dot_general(
                e.astype(bf16), za, nt, preferred_element_type=f32
            )
        both = jnp.concatenate([ot, dqt * scale], 0)
        out_ref[0, cols, 0 : 2 * hd] = both.T.astype(bf16)
    out_ref[0, :, 2 * hd : 4 * hd] = acc[...].astype(bf16)


def attention(x):
    n, length, width = x.shape
    hd = width // 4
    tq = 512 if length % 512 == 0 else 256
    tk = 512
    spec = pl.BlockSpec((1, length, width), lambda i: (i, 0, 0))
    return pl.pallas_call(
        partial(attention_kernel, length=length, hd=hd, tq=tq, tk=tk),
        grid=(n,),
        out_shape=jax.ShapeDtypeStruct(x.shape, bf16),
        in_specs=[spec],
        out_specs=spec,
        scratch_shapes=[
            pltpu.VMEM((width, length), bf16),
            pltpu.VMEM((length, 2 * hd), f32),
            pltpu.VMEM((length, tq), f32),
        ],
        compiler_params=pltpu.CompilerParams(vmem_limit_bytes=40 * 2**20),
        cost_estimate=pl.CostEstimate(
            flops=n * length * length * 4 * hd * 6, bytes_accessed=4 * n * length * width, transcendentals=n * length * length // 2
        ),
    )(x)


def exchange_attention(q, k, v, a):
    seqs, rows, inner = q.shape
    shards = lax.axis_size("seq")
    heads = inner // HEAD_DIM
    chunks = seqs * heads // shards
    wide = 4 * HEAD_DIM
    packed = jnp.stack([x.reshape(seqs, rows, heads, HEAD_DIM) for x in (q, k, v, a)], 3)
    packed = packed.reshape(seqs, rows, heads, wide).transpose(0, 2, 1, 3).reshape(chunks, shards, rows, wide)
    outs = []
    for c in range(chunks):
        mine = lax.all_to_all(packed[c], "seq", 0, 0, tiled=True)
        done = attention(mine.reshape(1, shards * rows, wide)).reshape(shards, rows, wide)
        outs.append(lax.all_to_all(done, "seq", 0, 0, tiled=True))
    back = jnp.concatenate(outs, 0).reshape(seqs, heads, rows, 4, HEAD_DIM).transpose(3, 0, 2, 1, 4)
    back = back.reshape(4, seqs, rows, inner)
    return back[0], back[1], back[2], back[3]


def ring_attention(q, k, v, a):
    seq_count, row_count, inner_width = q.shape
    score_scale = HEAD_DIM ** (-0.5)
    shard_total = lax.axis_size("seq")
    my_shard = lax.axis_index("seq")
    heads_of = lambda x: x.reshape(seq_count, row_count, inner_width // HEAD_DIM, HEAD_DIM)
    flat_of = lambda x: x.reshape(seq_count, row_count, inner_width)
    qh, gh = heads_of(q), heads_of(a)
    local = jnp.arange(row_count, dtype=jnp.int32)
    own_mask = local[:, None] >= local[None, :]
    ein = partial(jnp.einsum, preferred_element_type=f32)

    def attend_block(state, key_block, value_block, visible):
        running_max, exp_total, weighted = state
        raw = ein("sthd,suhd->shtu", qh, key_block) * score_scale
        raw = jnp.where(visible[None, None], raw, neg_big)
        new_max = jnp.maximum(running_max, jnp.max(raw, -1))
        weights = jnp.where(visible[None, None], jnp.exp(raw - new_max[..., None]), 0.0)
        shrink = jnp.exp(running_max - new_max)
        exp_total = exp_total * shrink + jnp.sum(weights, -1)
        weighted = weighted * jnp.transpose(shrink, (0, 2, 1))[..., None] + ein(
            "shtu,suhd->sthd", weights.astype(bf16), value_block
        )
        return (new_max, exp_total, weighted)

    head_count = inner_width // HEAD_DIM
    state = (
        jnp.full((seq_count, head_count, row_count), neg_big, f32),
        jnp.zeros((seq_count, head_count, row_count), f32),
        jnp.zeros(qh.shape, f32),
    )
    state = attend_block(state, heads_of(k), heads_of(v), own_mask)
    empty_stack = jnp.zeros((max(shard_total - 1, 1),) + q.shape, bf16)

    def forward_step(step, carry):
        state, near_keys, near_values, key_stack, value_stack = carry
        near_keys, near_values = passed_along((near_keys, near_values), "seq", 1)
        visible = jnp.broadcast_to(my_shard >= step, (row_count, row_count))
        state = attend_block(state, heads_of(near_keys), heads_of(near_values), visible)
        key_stack = lax.dynamic_update_index_in_dim(key_stack, near_keys, step - 1, 0)
        value_stack = lax.dynamic_update_index_in_dim(value_stack, near_values, step - 1, 0)
        return (state, near_keys, near_values, key_stack, value_stack)

    state, _, _, key_stack, value_stack = lax.fori_loop(
        1, shard_total, forward_step, (state, k, v, empty_stack, empty_stack)
    )
    running_max, exp_total, weighted = state
    log_total = running_max + jnp.log(exp_total)
    attended = weighted / jnp.transpose(exp_total, (0, 2, 1))[..., None]
    spread = jnp.transpose(jnp.sum(gh.astype(f32) * attended, -1), (0, 2, 1))

    def grads(key_block, value_block, visible):
        raw = ein("sthd,suhd->shtu", qh, key_block) * score_scale
        probs = jnp.where(visible[None, None], jnp.exp(raw - log_total[..., None]), 0.0)
        grad_probs = ein("sthd,suhd->shtu", gh, value_block)
        slopes = (probs * (grad_probs - spread[..., None])).astype(bf16)
        query_grad = ein("shtu,suhd->sthd", slopes, key_block) * score_scale
        key_grad = ein("shtu,sthd->suhd", slopes, qh) * score_scale
        value_grad = ein("shtu,sthd->suhd", probs.astype(bf16), gh)
        return query_grad, key_grad, value_grad

    d_query, d_keys, d_values = grads(heads_of(k), heads_of(v), own_mask)

    def return_step(index, carry):
        query_grad_total, travelling = carry
        step = shard_total - 1 - index
        near_keys = lax.dynamic_index_in_dim(key_stack, step - 1, 0, keepdims=False)
        near_values = lax.dynamic_index_in_dim(value_stack, step - 1, 0, keepdims=False)
        visible = jnp.broadcast_to(my_shard >= step, (row_count, row_count))
        query_grad, key_grad, value_grad = grads(heads_of(near_keys), heads_of(near_values), visible)
        joined = jnp.concatenate([flat_of(key_grad), flat_of(value_grad)], -1)
        travelling = passed_along((travelling + joined).astype(bf16), "seq", -1).astype(f32)
        return (query_grad_total + query_grad, travelling)

    start = jnp.zeros((seq_count, row_count, 2 * inner_width), f32)
    d_query, travelling = lax.fori_loop(0, shard_total - 1, return_step, (d_query, start))
    d_keys = flat_of(d_keys) + travelling[..., :inner_width]
    d_values = flat_of(d_values) + travelling[..., inner_width:]
    return tuple(x.astype(bf16) for x in (flat_of(attended), flat_of(d_query), d_keys, d_values))


def per_device(
    tokens, ln_gain, ln_bias, w_query, w_key, w_value, w_attn_out, w_in, b_in, w_mlp_out, b_out, cotangent
):
    x_low = tokens[0]
    cot = cotangent[0]
    seqs, rows, width = x_low.shape
    inner = w_query.shape[1]
    heads = inner // HEAD_DIM
    shards = lax.axis_size("seq")
    my_shard = lax.axis_index("seq")
    ein = partial(jnp.einsum, preferred_element_type=f32)
    positions = my_shard * rows + jnp.arange(rows, dtype=jnp.int32)
    tables = rotary_tables(positions, inner)
    x = x_low.astype(f32)
    centred = x - jnp.mean(x, -1, keepdims=True)
    inv_std = lax.rsqrt(jnp.mean(centred * centred, -1, keepdims=True) + epsilon)
    unit = centred * inv_std
    normed = (unit * ln_gain + ln_bias).astype(bf16)
    query = rotate(ein("std,de->ste", normed, w_query), tables, 1.0).astype(bf16)
    keys = rotate(ein("std,de->ste", normed, w_key), tables, 1.0).astype(bf16)
    values = ein("std,de->ste", normed, w_value).astype(bf16)
    d_attended = ein("std,ed->ste", cot, w_attn_out).astype(bf16)

    exchange = exchange_attention if (seqs * heads) % shards == 0 else ring_attention
    attended, d_query, d_keys, d_values = exchange(query, keys, values, d_attended)

    gate_in = ein("std,df->stf", normed, w_in) + b_in
    hidden, gelu_pull = jax.vjp(partial(jax.nn.gelu, approximate=True), gate_in)
    hidden = hidden.astype(bf16)
    d_hidden = ein("std,fd->stf", cot, w_mlp_out)
    d_gate = gelu_pull(d_hidden)[0].astype(bf16)
    d_b_in = jnp.sum(d_gate, (0, 1), dtype=f32)
    d_b_out = jnp.sum(cot, (0, 1), dtype=f32)
    d_w_mlp_out = ein("stf,std->fd", hidden, cot)
    d_w_in = ein("std,stf->df", normed, d_gate)
    mlp_part = ein("stf,fd->std", hidden, w_mlp_out)
    d_normed_mlp = ein("stf,df->std", d_gate, w_in)

    attn_part = ein("ste,ed->std", attended, w_attn_out)
    branches = lax.psum((attn_part + mlp_part).astype(bf16), "mlp").astype(f32)
    mixed = (x + branches + b_out).astype(bf16)
    d_w_attn_out = ein("ste,std->ed", attended, cot)
    d_query_pre = rotate(d_query.astype(f32), tables, -1.0).astype(bf16)
    d_key_pre = rotate(d_keys.astype(f32), tables, -1.0).astype(bf16)
    d_w_query = ein("std,ste->de", normed, d_query_pre)
    d_w_key = ein("std,ste->de", normed, d_key_pre)
    d_w_value = ein("std,ste->de", normed, d_values)
    d_normed_part = d_normed_mlp + ein("ste,de->std", d_query_pre, w_query)
    d_normed_part = d_normed_part + ein("ste,de->std", d_key_pre, w_key)
    d_normed_part = d_normed_part + ein("ste,de->std", d_values, w_value)
    d_normed = lax.psum(d_normed_part.astype(bf16), "mlp").astype(f32)
    d_gain = jnp.sum(d_normed * unit, (0, 1))
    d_bias = jnp.sum(d_normed, (0, 1))
    d_unit = d_normed * ln_gain
    d_inputs = inv_std * (
        d_unit - jnp.mean(d_unit, -1, keepdims=True) - unit * jnp.mean(d_unit * unit, -1, keepdims=True)
    )
    d_tokens = (cot.astype(f32) + d_inputs).astype(bf16)

    def total(v):
        return lax.psum(v.astype(bf16), "seq").astype(f32)

    return (
        mixed[None],
        d_tokens[None],
        total(d_gain),
        total(d_bias),
        total(d_w_query),
        total(d_w_key),
        total(d_w_value),
        total(d_w_attn_out),
        total(d_w_in),
        total(d_b_in),
        total(d_w_mlp_out),
        total(d_b_out),
    )


def solution(mesh):
    rows, whole = P("seq", None, None, None), P()
    cols, down = P(None, "mlp"), P("mlp", None)
    return jax.shard_map(
        per_device,
        mesh=mesh,
        in_specs=(rows, whole, whole, cols, cols, cols, down, cols, P("mlp"), down, whole, rows),
        out_specs=(rows, rows, whole, whole, cols, cols, cols, down, cols, P("mlp"), down, whole),
        check_vma=False,
    )
```

time: 797 us -> 436 us (0.55)
  matrix products: 170 us -> 56.2 us
  waiting for transfers between devices: 340 us -> 246 us
  starting transfers between devices: 104 us -> 18.3 us
  local copies, waits for them, and re-layouts: 74.8 us -> 20.2 us
  other arithmetic: 68.9 us -> 39.6 us
  Pallas kernels: 0 us -> 18.9 us
    dot_general x77 -> x18, matrix products: 170 us -> 56.2 us  [the longest x1 8.37 us: per_device(): d_hidden = ein('std,fd->stf', cot, w_mlp_out)]
    ppermute x21 -> x0, starting transfers between devices: 104 us -> none  [passed_along(): return lax.ppermute(x, axis, pairs)]
    ppermute x21 -> x0, waiting for transfers between devices: 79 us -> none  [passed_along(): return lax.ppermute(x, axis, pairs)]
    while x105 -> x0, local copies, waits for them, and re-layouts: 31.1 us -> none
    psum x2, waiting for transfers between devices: 261 us -> 233 us  [the longest x1 146 us: per_device(): branches = lax.psum((attn_part + mlp_part).astype(bf16), 'mlp').astype(f32)]
    convert_element_type x25 -> x13, other arithmetic: 41.6 us -> 16.2 us  [the longest x10 14.8 us: total(): return lax.psum(v.astype(bf16), 'seq').astype(f32)]
    dynamic_update_slice x14 -> x0, local copies, waits for them, and re-layouts: 19 us -> none  [the longest x7 13.2 us: forward_step(): lax.dynamic_update_index_in_dim(value_stack, near_values, step - 1, 0)]
    pallas_call x0 -> x2, Pallas kernels: none -> 18.9 us  [attention(): pl.pallas_call(partial(attention_kernel, length=length, hd=hd, tq=tq, tk=...]
  transfers between devices with their start and end apart: 23 -> 6, of which waited for: 9 -> 4; matrix products, arithmetic and copies ran while one was open for 8% -> 15% of each run, Pallas kernels for 0% -> 4%
where the time goes in v1:
time: 436 us; the launch traced here: 428 us
  waiting for transfers between devices  246 us (56%)
  matrix products  56.2 us (13%)
  other arithmetic  39.6 us (9%)
  local copies, waits for them, and re-layouts  20.2 us (5%)
  Pallas kernels  18.9 us (4%)
  starting transfers between devices  18.3 us (4%)
  between operations  15.2 us (3%)
  blocking collectives  13.9 us (3%)
    psum x1, waiting for transfers between devices, per_device(): branches = lax.psum((attn_part + mlp_part).astype(bf16), 'mlp').astype(f32)  146 us
    psum x1, waiting for transfers between devices, total(): return lax.psum(v.astype(bf16), 'seq').astype(f32)  86.9 us
    pallas_call x2, Pallas kernels, attention(): pl.pallas_call(partial(attention_kernel, length=length, hd=hd, tq=tq, tk=...  18.9 us
    convert_element_type x10, other arithmetic, total(): return lax.psum(v.astype(bf16), 'seq').astype(f32)  14.8 us
    psum x1, blocking collectives, total(): return lax.psum(v.astype(bf16), 'seq').astype(f32)  13.9 us
    all_to_all x2, starting transfers between devices, exchange_attention(): mine = lax.all_to_all(packed[c], 'seq', 0, 0, tiled=True)  9.19 us
  transfers between devices with their start and end apart: 6, of which 4 were waited for; matrix products, arithmetic and copies ran while one was open for 15% of the time, Pallas kernels for 4%

profile of v1, /device:TPU:0, one launch (start us, length us, event | category | flops | bytes accessed | tf_op | source)
XLA Modules:
  0.0 427.8 jit_solution(10924994233022004228)
XLA Ops:
  7.3 2.1 convert_reduce_fusion
  9.4 2.3 fusion.15
  11.7 1.3 fusion.72
  13.0 1.3 fusion.75
  14.3 0.9 copy-done.9
  15.2 2.1 fusion.121
  17.4 3.0 convolution_convert_fusion
  20.5 0.7 fusion.56
  21.3 1.1 fusion.89
  22.4 0.6 fusion.61
  23.3 1.1 fusion.115
  24.5 1.3 copy.49
  25.8 5.2 %all-to-all-start.2 = ((bf16[8,256,256]{2,1,0:T(8,128)(2,1)}), bf16[8,256,256]{2,1,0:T(8,128)(2,1)S(1)}, u32[]{:S(2)}, u32[]{:S(2)}) async-start(bf16[8,256,256]{2,1,0:T(8,128)(2,1)} %copy.49), calls=%async_computation.2 | async-start | bytes 2097152 | tf_op jit(solution)/shard_map/all_to_all | solution.py:132
  30.9 2.3 copy.47
  33.2 6.6 %fusion.39 = f32[4,256,1024]{2,1,0:T(8,128)} fusion(bf16[1024,1024]{1,0:T(8,128)(2,1)} %param.19, bf16[1,4,256,1024]{3,2,1,0:T(8,128)(2,1)} %param.12, f32[1024]{0:T(1024)S(1)} %copy-done.48, f32[1024]{0:T(1024)S(1)} %copy-done.46, f32[4,256]{1,0:T(4,128)S(1)} %add_rsqrt_fusion, f32[4,256]{1,0:T(4,128)S(1)} %broadcast_multiply_fusion.2), kind=kOutput, calls=%fused_computation.53 | convolution fusion | flops 2153775104 | bytes 8404992 | tf_op jit(solution)/shard_map/std,df->stf/dot_general | solution.py:247
  39.8 6.5 %all-to-all-done.2 = bf16[8,256,256]{2,1,0:T(8,128)(2,1)S(1)} async-done(((bf16[8,256,256]{2,1,0:T(8,128)(2,1)}), bf16[8,256,256]{2,1,0:T(8,128)(2,1)S(1)}, u32[]{:S(2)}, u32[]{:S(2)}) %all-to-all-start.2) | async-done | bytes 1048608 | tf_op jit(solution)/shard_map/all_to_all | solution.py:132
  46.3 1.0 copy-done.1
  47.3 4.0 all-to-all-start
  51.4 8.4 %fusion.124 = (bf16[1024]{0:T(1024)(128)(2,1)S(1)}, bf16[4,256,1024]{2,1,0:T(8,128)(2,1)}) fusion(f32[4,256,1024]{2,1,0:T(8,128)} %fusion.39, f32[1024]{0:T(1024)S(1)} %copy-done.49, bf16[1024,1024]{1,0:T(8,128)(2,1)S(1)} %copy-done, bf16[1,4,256,1024]{3,2,1,0:T(8,128)(2,1)} %param.23), kind=kOutput, calls=%fused_computation.171 | convolution fusion | flops 2170551296 | bytes 10491904 | tf_op jit(solution)/shard_map/std,fd->stf/dot_general | solution.py:250
  59.7 9.4 %shard_map.212 = bf16[1,2048,256]{2,1,0:T(8,128)(2,1)S(1)} custom-call(bf16[1,2048,256]{2,1,0:T(8,128)(2,1)S(1)} %bitcast.182), custom_call_target="tpu_custom_call" | custom-call | flops 6442450944 | bytes 2097152 | tf_op jit(solution)/shard_map/pallas_call | solution.py:104
  69.2 1.0 copy-done.3
  70.2 2.3 copy.50
  72.4 4.4 %all-to-all-start.3 = ((bf16[8,256,256]{1,2,0:T(8,128)(2,1)}), bf16[8,256,256]{1,2,0:T(8,128)(2,1)}, u32[]{:S(2)}, u32[]{:S(2)}) async-start(bf16[8,256,256]{1,2,0:T(8,128)(2,1)} %copy.50), calls=%async_computation.3 | async-start | bytes 2097152 | tf_op jit(solution)/shard_map/all_to_all | solution.py:134
  76.9 6.2 %bitcast_convert_fusion.1 = bf16[1024,1024]{1,0:T(8,128)(2,1)} fusion(bf16[4,256,1024]{2,1,0:T(8,128)(2,1)} %get-tuple-element.62, bf16[1,4,256,1024]{3,2,1,0:T(8,128)(2,1)} %param.12, f32[1024]{0:T(1024)S(1)} %copy-done.48, f32[1024]{0:T(1024)S(1)} %copy-done.46, f32[4,256]{1,0:T(4,128)S(1)} %add_rsqrt_fusion, f32[4,256]{1,0:T(4,128)S(1)} %broadcast_multiply_fusion.2), kind=kOutput, calls=%fused_computation.39 | convolution fusion | flops 2154823680 | bytes 6307840 | tf_op jit(solution)/shard_map/std,stf->df/dot_general | solution.py:255
  83.1 9.4 %shard_map.211 = bf16[1,2048,256]{2,1,0:T(8,128)(2,1)S(1)} custom-call(bf16[1,2048,256]{2,1,0:T(8,128)(2,1)S(1)} %bitcast.181), custom_call_target="tpu_custom_call" | custom-call | flops 6442450944 | bytes 2097152 | tf_op jit(solution)/shard_map/pallas_call | solution.py:104
  92.6 1.0 copy-done.4
  93.6 2.3 copy.48
  95.8 4.2 all-to-all-start.1
  100.2 2.0 fusion.94
  102.2 7.2 %bitcast_convert_fusion = bf16[1024,1024]{1,0:T(8,128)(2,1)} fusion(bf16[1,4,256,1024]{3,2,1,0:T(8,128)(2,1)} %param.23, f32[4,256,1024]{2,1,0:T(8,128)} %fusion.39, f32[1024]{0:T(1024)S(1)} %copy-done.49), kind=kOutput, calls=%fused_computation.38 | convolution fusion | flops 2159017984 | bytes 8392704 | tf_op jit(solution)/shard_map/stf,std->fd/dot_general | solution.py:254
  109.5 5.9 %all-to-all-done.1 = bf16[8,256,256]{1,2,0:T(8,128)(2,1)S(1)} async-done(((bf16[8,256,256]{1,2,0:T(8,128)(2,1)}), bf16[8,256,256]{1,2,0:T(8,128)(2,1)S(1)}, u32[]{:S(2)}, u32[]{:S(2)}) %all-to-all-start.1) | async-done | bytes 1048608 | tf_op jit(solution)/shard_map/all_to_all | solution.py:134
  115.4 1.4 pad_maximum_fusion.1
  117.5 0.6 copy-done.7
  118.2 1.2 copy-done.6
  119.5 2.0 fusion.52
  121.5 1.5 fusion.53
  123.5 0.5 copy-done.35
  124.4 0.7 add_convert_fusion.2
  125.2 2.0 fusion.51
  127.2 2.0 fusion.50
  129.5 4.7 %fusion.37 = f32[4,256,1024]{2,1,0:T(8,128)S(1)} fusion(bf16[4,256,1024]{2,1,0:T(8,128)(2,1)} %get-tuple-element.62, bf16[1024,1024]{1,0:T(8,128)(2,1)} %param.19), kind=kOutput, calls=%fused_computation.51 | convolution fusion | flops 2147483648 | bytes 8388608 | tf_op jit(solution)/shard_map/stf,df->std/dot_general | solution.py:257
  134.3 2.8 fusion.35
  137.2 2.1 add_convert_fusion.1
  140.1 1.1 fusion.65
  141.3 0.3 copy-done.14
  141.8 1.1 fusion.66
  143.0 2.1 add_convert_fusion
  145.2 2.0 reduce_sum.88
  147.1 86.9 %all-reduce.6.cloned.1.call-done = (bf16[1024,256]{1,0:T(8,128)(2,1)}, bf16[1024,256]{1,0:T(8,128)(2,1)}, bf16[1024,256]{1,0:T(8,128)(2,1)}, bf16[256,1024]{1,0:...) async-done(((bf16[1024,256]{1,0:T(8,128)(2,1)}, bf16[1024,256]{1,0:T(8,128)(2,1)}, bf16[1024,256]{1,0:T(8,128)(2,1)}, bf16[256,1024]{1,0:T(8,128)(2,1)}, ...) | async-done | bytes 6291472 | tf_op jit(solution)/shard_map/psum | solution.py:281
  234.0 2.2 convert_element_type.199
  236.3 2.1 convert_element_type.204
  238.4 2.1 convert_element_type.206
  240.5 1.1 convert_element_type.208
  241.5 2.5 convert_element_type.210
  244.0 2.5 convert_element_type.213
  246.5 146.1 %all-reduce.8.cloned.1.call-done = (bf16[4,256,1024]{2,1,0:T(8,128)(2,1)}, bf16[4,256,1024]{2,1,0:T(8,128)(2,1)}) async-done(((bf16[4,256,1024]{2,1,0:T(8,128)(2,1)}, bf16[4,256,1024]{2,1,0:T(8,128)(2,1)}), (bf16[4,256,1024]{2,1,0:T(8,128)(2,1)}, bf16[4,256,1024]{2,1,0:T(8,128)(2,1)})) %all-reduce.8.cloned.1.call-update) | async-done | bytes 4194320 | tf_op jit(solution)/shard_map/psum | solution.py:260
  392.7 2.0 reduce_sum.86
  394.6 3.8 fusion.17
  398.4 13.9 %all-reduce = (bf16[1024]{0:T(1024)(128)(2,1)S(1)}, bf16[1024]{0:T(1024)(128)(2,1)S(1)}, bf16[1024]{0:T(1024)(128)(2,1)S(1)}, bf16[1024]{0:T(1024)(128)(2,1)S(1)}) all-reduce(bf16[1024]{0:T(1024)(128)(2,1)S(1)} %get-tuple-element.12, bf16[1024]{0:T(1024)(128)(2,1)S(1)} %reduce_sum.86, ...), channel_id=1, replica_groups=mesh['seq'=8,'mlp'=4] {'seq'}, use_global_device_ids=true, to_apply=%region_7.8 | all-reduce | flops 4096 | bytes 16384 | tf_op jit(solution)/shard_map/psum | solution.py:281
  412.3 0.6 convert_element_type.190
  412.9 0.6 convert_element_type.191
  413.5 0.6 convert_element_type.211
  414.1 0.6 convert_element_type.214
  414.7 5.9 %fusion.33 = (bf16[1,4,256,1024]{3,2,1,0:T(8,128)(2,1)}, bf16[1,4,256,1024]{3,2,1,0:T(8,128)(2,1)}) fusion(bf16[1,4,256,1024]{3,2,1,0:T(8,128)(2,1)} %param.12, bf16[4,256,1024]{2,1,0:T(8,128)(2,1)} %get-tuple-element.26, bf16[1,4,256,1024]{3,2,1,0:T(8,128)(2,1)} %param.23, f32[4,256]{1,0:T(4,128)S(1)} %broadcast_multiply_fusion, ...), kind=kLoop, calls=%fused_computation.45 | loop fusion | flops 16777216 | bytes 12607488 | tf_op jit(solution)/shard_map/broadcast_in_dim | solution.py:285
  (120 shorter events, 4.0 us)
Async XLA Ops:
  7.2 44.2 %copy-start = (bf16[1024,1024]{1,0:T(8,128)(2,1)S(1)}, bf16[1024,1024]{1,0:T(8,128)(2,1)}, u32[]{:S(2)}) copy-start(bf16[1024,1024]{1,0:T(8,128)(2,1)} %param.21) | copy-start | bytes 6291460
  7.2 4.5 %copy-start.5 = (bf16[1,4,256,1024]{3,2,1,0:T(8,128)(2,1)S(1)}, bf16[1,4,256,1024]{3,2,1,0:T(8,128)(2,1)}, u32[]{:S(2)}) copy-start(bf16[1,4,256,1024]{3,2,1,0:T(8,128)(2,1)} %param.12) | copy-start | bytes 6291460
  7.2 4.5 %copy-start.46 = (f32[1024]{0:T(1024)S(1)}, f32[1024]{0:T(1024)}, u32[]{:S(2)}) copy-start(f32[1024]{0:T(1024)} %param.13) | copy-start | bytes 12292
  7.2 4.5 %copy-start.48 = (f32[1024]{0:T(1024)S(1)}, f32[1024]{0:T(1024)}, u32[]{:S(2)}) copy-start(f32[1024]{0:T(1024)} %param.14) | copy-start | bytes 12292
  7.2 4.5 %copy-start.42 = (bf16[1024,256]{1,0:T(8,128)(2,1)S(1)}, bf16[1024,256]{1,0:T(8,128)(2,1)}, u32[]{:S(2)}) copy-start(bf16[1024,256]{1,0:T(8,128)(2,1)} %param.16) | copy-start | bytes 1572868
  11.7 1.3 copy-start.40
  14.3 1.0 copy-start.9
  17.4 3.1 copy-start.19
  17.4 3.1 copy-start.38
  17.4 5.0 %copy-start.10 = (f32[4,256,256]{1,2,0:T(8,128)S(1)}, f32[4,256,256]{1,2,0:T(8,128)}, u32[]{:S(2)}) copy-start(f32[4,256,256]{1,2,0:T(8,128)} %copy-done.9) | copy-start | bytes 3145732
  17.4 5.0 %copy-start.25 = (f32[4,256,255]{1,2,0:T(8,128)S(1)}, f32[4,256,255]{1,2,0:T(8,128)}, u32[]{:S(2)}) copy-start(f32[4,256,255]{1,2,0:T(8,128)} %get-tuple-element.47) | copy-start | bytes 3133444
  17.4 5.0 %copy-start.26 = (f32[4,256,255]{1,2,0:T(8,128)S(1)}, f32[4,256,255]{1,2,0:T(8,128)}, u32[]{:S(2)}) copy-start(f32[4,256,255]{1,2,0:T(8,128)} %get-tuple-element.48) | copy-start | bytes 3133444
  17.4 5.0 %copy-start.27 = (f32[4,256,255]{1,2,0:T(8,128)S(1)}, f32[4,256,255]{1,2,0:T(8,128)}, u32[]{:S(2)}) copy-start(f32[4,256,255]{1,2,0:T(8,128)} %get-tuple-element.67) | copy-start | bytes 3133444
  17.4 5.0 %copy-start.28 = (f32[4,256,255]{1,2,0:T(8,128)S(1)}, f32[4,256,255]{1,2,0:T(8,128)}, u32[]{:S(2)}) copy-start(f32[4,256,255]{1,2,0:T(8,128)} %get-tuple-element.68) | copy-start | bytes 3133444
  22.4 1.0 copy-start.21
  22.4 1.0 copy-start.23
  25.8 20.6 %all-to-all-start.2 = ((bf16[8,256,256]{2,1,0:T(8,128)(2,1)}), bf16[8,256,256]{2,1,0:T(8,128)(2,1)S(1)}, u32[]{:S(2)}, u32[]{:S(2)}) async-start(bf16[8,256,256]{2,1,0:T(8,128)(2,1)} %copy.49), calls=%async_computation.2 | async-start | bytes 2097152 | tf_op jit(solution)/shard_map/all_to_all | solution.py:132
  33.2 18.2 %copy-start.49 = (f32[1024]{0:T(1024)S(1)}, f32[1024]{0:T(1024)}, u32[]{:S(2)}) copy-start(f32[1024]{0:T(1024)} %param.20) | copy-start | bytes 12292
  46.3 1.0 copy-start.1
  47.3 25.1 %all-to-all-start = ((bf16[8,256,256]{2,1,0:T(8,128)(2,1)}), bf16[8,256,256]{2,1,0:T(8,128)(2,1)S(1)}, u32[]{:S(2)}, u32[]{:S(2)}) async-start(bf16[8,256,256]{2,1,0:T(8,128)(2,1)} %copy.47), calls=%async_computation | async-start | bytes 2097152 | tf_op jit(solution)/shard_map/all_to_all | solution.py:132
  51.4 8.4 %copy-start.2 = (bf16[8,256,256]{2,1,0:T(8,128)(2,1)S(1)}, bf16[8,256,256]{2,1,0:T(8,128)(2,1)}, u32[]{:S(2)}) copy-start(bf16[8,256,256]{2,1,0:T(8,128)(2,1)} %copy-done.1) | copy-start | bytes 3145732
  69.2 1.0 copy-start.3
  72.4 23.4 %all-to-all-start.3 = ((bf16[8,256,256]{1,2,0:T(8,128)(2,1)}), bf16[8,256,256]{1,2,0:T(8,128)(2,1)}, u32[]{:S(2)}, u32[]{:S(2)}) async-start(bf16[8,256,256]{1,2,0:T(8,128)(2,1)} %copy.50), calls=%async_computation.3 | async-start | bytes 2097152 | tf_op jit(solution)/shard_map/all_to_all | solution.py:134
  92.6 1.0 copy-start.4
  95.8 19.6 %all-to-all-start.1 = ((bf16[8,256,256]{1,2,0:T(8,128)(2,1)}), bf16[8,256,256]{1,2,0:T(8,128)(2,1)S(1)}, u32[]{:S(2)}, u32[]{:S(2)}) async-start(bf16[8,256,256]{1,2,0:T(8,128)(2,1)} %copy.48), calls=%async_computation.1 | async-start | bytes 2097152 | tf_op jit(solution)/shard_map/all_to_all | solution.py:134
  100.0 134.1 %all-reduce.6.cloned.1.call-start = ((), (), s32[]{:S(2)}) async-start(), calls=%async_computation.4 | async-start | bytes 12582912 | tf_op jit(solution)/shard_map/psum | solution.py:281
  117.1 1.0 copy-start.7
  117.1 1.1 copy-start.33
  117.1 4.4 %copy-start.29 = (bf16[1,4,256,4,64]{2,4,0,3,1:T(8,128)(2,1)}, bf16[1,4,256,4,64]{2,4,0,3,1:T(8,128)(2,1)S(1)}, u32[]{:S(2)}) copy-start(bf16[1,4,256,4,64]{2,4,0,3,1:T(8,128)(2,1)S(1)} %get-tuple-element.34) | copy-start | bytes 1572868
  117.1 2.3 copy-start.6
  118.1 3.4 copy-start.20
  123.0 0.9 copy-start.35
  123.0 1.1 copy-start.36
  123.0 1.4 copy-start.37
  123.1 2.0 copy-start.11
  123.2 1.9 copy-start.13
  123.3 1.8 copy-start.15
  123.4 3.7 copy-start.17
  129.2 263.4 %all-reduce.8.cloned.1.call-start = ((), (), s32[]{:S(2)}) async-start(), calls=%async_computation.5 | async-start | bytes 8388608 | tf_op jit(solution)/shard_map/psum | solution.py:260
  129.5 4.8 %copy-start.50 = (f32[4,256,1024]{2,1,0:T(8,128)S(1)}, f32[4,256,1024]{2,1,0:T(8,128)}, u32[]{:S(2)}) copy-start(f32[4,256,1024]{2,1,0:T(8,128)} %fusion.39) | copy-start | bytes 12582916
  134.3 2.8 copy-start.30
  134.3 2.8 copy-start.39
  137.1 2.1 copy-start.8
  137.1 2.1 copy-start.16
  137.2 2.1 copy-start.18
  137.2 2.3 copy-start.22
  137.2 2.6 copy-start.24
  137.2 2.9 copy-start.41
  140.0 1.3 copy-start.12
  140.0 1.6 copy-start.14
  140.1 1.7 copy-start.43
  141.8 1.1 copy-start.34
  141.8 1.2 copy-start.44
  234.0 6.4 %copy-start.45 = (bf16[256,1024]{1,0:T(8,128)(2,1)S(1)}, bf16[256,1024]{1,0:T(8,128)(2,1)}, u32[]{:S(2)}) copy-start(bf16[256,1024]{1,0:T(8,128)(2,1)} %get-tuple-element.22) | copy-start | bytes 1572868
  234.0 7.5 %copy-start.32 = (bf16[1024,1024]{1,0:T(8,128)(2,1)S(1)}, bf16[1024,1024]{1,0:T(8,128)(2,1)}, u32[]{:S(2)}) copy-start(bf16[1024,1024]{1,0:T(8,128)(2,1)} %get-tuple-element.23) | copy-start | bytes 6291460
  240.4 3.6 copy-start.31
  246.5 168.2 %copy-start.47 = (f32[1024]{0:T(1024)S(1)}, f32[1024]{0:T(1024)}, u32[]{:S(2)}) copy-start(f32[1024]{0:T(1024)} %param.22) | copy-start | bytes 12292
Sparse Core Ops, SparseCore 0:
  129.3 104.6 all-reduce.5
  237.1 155.4 all-reduce.7
